TPU v7x, 32 devices: a whole 2x2x4 slice. The times are simulated.
32 devices in a mesh: query: 2 (over x), corpus: 16 (over z, y, core).
Axes of the slice: x: 2, y: 2, z: 4, core: 2. Of those that a mesh axis runs over, the one named last changes fastest.
Arguments:
- clean_feats: bfloat16 [2, 2, 512, 320], P('query', None, 'corpus'), may hold values from -6 to 6
- noise_draw: bfloat16 [2, 2, 512, 320], P('query', None, 'corpus'), may hold values from -6 to 6
- timesteps: int32 [2, 2], P('query'), may hold values from 0 to 999
- weight_in: bfloat16 [2, 320, 320], P(None, None, 'corpus'), may hold values from -0.3125 to 0.3125
- weight_ffin: bfloat16 [2, 320, 2560], P(None, None, 'corpus'), may hold values from -0.3125 to 0.3125
- weight_ffout: bfloat16 [2, 1280, 320], P(None, None, 'corpus'), may hold values from -0.15625 to 0.15625
- weight_out: bfloat16 [2, 320, 320], P(None, None, 'corpus'), may hold values from -0.3125 to 0.3125
- norm_gain: float32 [2, 320], replicated, may hold values from 0.5 to 1.5
- norm_bias: float32 [2, 320], replicated, may hold values from -3 to 3
- sketch_cin: bfloat16 [2, 3, 320, 16], replicated, may hold values from -0.3125 to 0.3125
- sketch_fin: bfloat16 [2, 1280, 16], replicated, may hold values from -0.15625 to 0.15625
- sketch_cout: bfloat16 [2, 3, 320, 16], replicated, may hold values from -0.3125 to 0.3125
- sketch_fout: bfloat16 [2, 2560, 16], replicated, may hold values from -0.125 to 0.125
- precond: float32 [8, 256, 256], P('query'), as said below
- store_grads: bfloat16 [8192, 2048], P(('query', 'corpus')), may hold values from -6 to 6
- store_scale: float32 [8192], P(('query', 'corpus')), may hold values from 0.002 to 0.03
Outputs:
- scores: float32 [2, 8192], P(None, ('query', 'corpus'))
Inputs may be any that keep to these rules, and one draw needn't show every extreme that they name: `precond`: each layer's matrix is symmetric with a diagonal between 1 and 2.
All inputs are finite; a program needn't handle non-finite values.
Results may differ from a plain program's by a relative error of at most 0.0085.
Values may be sent and summed in bfloat16 or wider, within the bound.
A program may use at most 64 MiB of HBM per device.

v0:
```python
import math
import jax
import jax.numpy as jnp
from jax import lax
from jax.sharding import PartitionSpec as P

plan_len = 1000


def noise_levels(timesteps):
    steps = jnp.arange(plan_len, dtype=jnp.float32)
    rooted = math.sqrt(0.00085) + (math.sqrt(0.012) - math.sqrt(0.00085)) * steps / (plan_len - 1)
    cumulative = jnp.exp(jnp.cumsum(jnp.log1p(-rooted * rooted)))
    matches = timesteps[..., None] == jnp.arange(plan_len, dtype=jnp.int32)
    picked = jnp.sum(jnp.where(matches, cumulative, jnp.zeros_like(cumulative)), axis=-1)
    return (jnp.sqrt(picked), jnp.sqrt(1.0 - picked))


def gelu_parts(gate):
    cumul = 0.5 * (1.0 + jax.scipy.special.erf(gate / math.sqrt(2.0)))
    density = jnp.exp(-0.5 * gate * gate) / math.sqrt(2.0 * math.pi)
    return (gate * cumul, cumul + gate * density)


def contract_back(delta, weight):
    return lax.dot_general(
        delta, weight, (((1,), (1,)), ((), ())), preferred_element_type=jnp.float32
    )


def block_forward(residual_stream, weights, scale_gain, shift_bias):
    weight_in, weight_ffin, weight_ffout, weight_out = weights
    hidden = weight_ffout.shape[0]
    residual_reduced = residual_stream.astype(jnp.bfloat16)
    inner = jnp.dot(residual_reduced, weight_in, preferred_element_type=jnp.float32)
    centred_input = inner - jnp.mean(inner, axis=-1, keepdims=True)
    inverse_deviation = lax.rsqrt(
        jnp.mean(centred_input * centred_input, axis=-1, keepdims=True) + 1e-05
    )
    standardized_input = centred_input * inverse_deviation
    normalized_input = (standardized_input * scale_gain + shift_bias).astype(jnp.bfloat16)
    projected = jnp.dot(normalized_input, weight_ffin, preferred_element_type=jnp.float32)
    value_output = projected[:, :hidden]
    gate = projected[:, hidden:]
    gelu_result, gelu_derivative = gelu_parts(gate)
    mixed_hidden = (value_output * gelu_result).astype(jnp.bfloat16)
    inner_two = inner + jnp.dot(mixed_hidden, weight_ffout, preferred_element_type=jnp.float32)
    inner_reduced = inner_two.astype(jnp.bfloat16)
    residual_stream = residual_stream + jnp.dot(
        inner_reduced, weight_out, preferred_element_type=jnp.float32
    )
    return (
        residual_stream,
        (
            residual_reduced,
            standardized_input,
            inverse_deviation,
            normalized_input,
            value_output,
            gelu_result,
            gelu_derivative,
            mixed_hidden,
            inner_reduced,
        ),
    )


def block_backward(dstream, saved_activations, weights, scale_gain):
    weight_in, weight_ffin, weight_ffout, weight_out = weights
    (
        residual_reduced,
        standardized_input,
        inverse_deviation,
        normalized_input,
        value_output,
        gelu_result,
        gelu_derivative,
        mixed_hidden,
        inner_reduced,
    ) = saved_activations
    dout_low = dstream.astype(jnp.bfloat16)
    second_inner_gradient = contract_back(dout_low, weight_out)
    dtwo_low = second_inner_gradient.astype(jnp.bfloat16)
    dmixed = contract_back(dtwo_low, weight_ffout)
    dproj_low = jnp.concatenate(
        [dmixed * gelu_result, dmixed * value_output * gelu_derivative], axis=-1
    ).astype(jnp.bfloat16)
    dnormed = contract_back(dproj_low, weight_ffin)
    scaled_hidden = dnormed * scale_gain
    inner_gradient = second_inner_gradient + inverse_deviation * (
        scaled_hidden
        - jnp.mean(scaled_hidden, axis=-1, keepdims=True)
        - standardized_input * jnp.mean(scaled_hidden * standardized_input, axis=-1, keepdims=True)
    )
    dinner_low = inner_gradient.astype(jnp.bfloat16)
    dstream = dstream + contract_back(dinner_low, weight_in)
    records = [
        (residual_reduced, dinner_low),
        (normalized_input, dproj_low),
        (mixed_hidden, dtwo_low),
        (inner_reduced, dout_low),
    ]
    return (dstream, records)


def project_layer(inputs, deltas, sketch_in, sketch_out, samples):
    left = jnp.dot(inputs, sketch_in, preferred_element_type=jnp.float32)
    right = jnp.dot(deltas, sketch_out, preferred_element_type=jnp.float32)
    left = left.reshape(samples, -1, left.shape[-1])
    right = right.reshape(samples, -1, right.shape[-1])
    outer = jnp.einsum("srk,srj->skj", left, right, precision=lax.Precision.HIGHEST)
    return outer.reshape(samples, -1)


def sketches_of(block, sketch_cin, sketch_fin, sketch_cout, sketch_fout):
    return [
        (sketch_cin[block, 0], sketch_cout[block, 0]),
        (sketch_cin[block, 1], sketch_fout[block]),
        (sketch_fin[block], sketch_cout[block, 1]),
        (sketch_cin[block, 2], sketch_cout[block, 2]),
    ]


def on_device(
    clean_feats,
    noise_draw,
    timesteps,
    weight_in,
    weight_ffin,
    weight_ffout,
    weight_out,
    norm_gain,
    norm_bias,
    sketch_cin,
    sketch_fin,
    sketch_cout,
    sketch_fout,
    precond,
    store_grads,
    store_scale,
):
    samples = clean_feats.shape[0]
    positions = clean_feats.shape[2] * lax.axis_size("corpus")
    loss_scale = 1.0 / math.sqrt(clean_feats.shape[1] * positions)
    blocks = weight_in.shape[0]
    signal, spread = noise_levels(timesteps)
    noise_rows = noise_draw.astype(jnp.float32)
    residual_stream = (
        signal[:, :, None, None] * clean_feats.astype(jnp.float32)
        + spread[:, :, None, None] * noise_rows
    )
    residual_stream = residual_stream.reshape(-1, residual_stream.shape[-1])
    noise_rows = noise_rows.reshape(-1, noise_rows.shape[-1])
    gathered = (
        lax.all_gather(weight_in, "corpus", axis=2, tiled=True),
        lax.all_gather(weight_ffin, "corpus", axis=2, tiled=True),
        lax.all_gather(weight_ffout, "corpus", axis=2, tiled=True),
        lax.all_gather(weight_out, "corpus", axis=2, tiled=True),
    )

    def fetch_forward(block):
        return tuple((member[block] for member in gathered))

    def fetch_backward(block):
        return tuple((member[block] for member in gathered))

    saved_all = []
    for block in range(blocks):
        residual_stream, saved_activations = block_forward(
            residual_stream, fetch_forward(block), norm_gain[block], norm_bias[block]
        )
        saved_all.append(saved_activations)
    dstream = (residual_stream - noise_rows) * loss_scale
    layers = [None] * (4 * blocks)
    for block in reversed(range(blocks)):
        dstream, records = block_backward(
            dstream, saved_all[block], fetch_backward(block), norm_gain[block]
        )
        pairs = sketches_of(block, sketch_cin, sketch_fin, sketch_cout, sketch_fout)
        for index in range(4):
            layers[4 * block + index] = project_layer(
                records[index][0], records[index][1], pairs[index][0], pairs[index][1], samples
            )
    partial_grads = jnp.stack(layers, axis=1)
    totals = lax.psum(partial_grads, "corpus")
    routed = lax.all_to_all(totals, "query", split_axis=1, concat_axis=0, tiled=True)
    owned = jnp.einsum("qlk,lkj->qlj", routed, precond, precision=lax.Precision.HIGHEST).astype(
        jnp.bfloat16
    )
    preconditioned = lax.all_gather(owned, "query", axis=1, tiled=True)
    flat = preconditioned.reshape(preconditioned.shape[0], -1)
    raw = lax.dot_general(
        flat, store_grads, (((1,), (1,)), ((), ())), preferred_element_type=jnp.float32
    )
    return raw * store_scale[None, :]


def solution(mesh):
    placed = (
        P("query", None, "corpus", None),
        P("query", None, "corpus", None),
        P("query", None),
        P(None, None, "corpus"),
        P(None, None, "corpus"),
        P(None, None, "corpus"),
        P(None, None, "corpus"),
        P(),
        P(),
        P(),
        P(),
        P(),
        P(),
        P("query", None, None),
        P(("query", "corpus"), None),
        P(("query", "corpus")),
    )
    return jax.shard_map(
        on_device,
        mesh=mesh,
        in_specs=placed,
        out_specs=P(None, ("query", "corpus")),
        check_vma=False,
    )
```

profile of v0, /device:TPU:0, one launch (start us, length us, event | category | flops | bytes accessed | tf_op | source)
XLA Modules:
  0.0 166.5 jit_solution(25093315047385760)
XLA Ops:
  6.5 0.7 all-gather.5.cloned.1.call-update
  7.3 0.7 all-gather.3.cloned.1.call-update
  8.4 24.9 %all_gather.15 = bf16[2,320,320]{1,0,2:T(2,128)(2,1)S(1)} all-gather(bf16[2,320,20]{1,0,2:T(2,128)(2,1)} %param.19), channel_id=1, replica_groups=mesh['query'=2,'corpus'=16] {'corpus'}, dimensions={2}, use_global_device_ids=true | all-gather | bytes 435200 | tf_op jit(solution)/shard_map/all_gather | solution.py:155
  33.3 0.7 fusion.105
  34.0 0.9 copy.52
  34.9 20.2 %all_gather.18 = bf16[2,320,320]{1,0,2:T(2,128)(2,1)S(1)} all-gather(bf16[2,320,20]{1,0,2:T(2,128)(2,1)S(1)} %copy-done.12), channel_id=1, replica_groups=mesh['query'=2,'corpus'=16] {'corpus'}, dimensions={2}, use_global_device_ids=true | all-gather | bytes 435200 | tf_op jit(solution)/shard_map/all_gather | solution.py:158
  55.1 0.7 fusion.104
  55.8 0.9 copy.54
  56.7 0.9 copy.55
  57.6 0.9 copy.57
  58.6 0.6 slice_reduce_fusion.1
  59.5 0.7 fusion.102
  60.7 0.8 fusion.79
  61.7 0.6 copy-done.4
  62.3 0.8 fusion.76
  63.2 5.7 %fusion.103 = (bf16[1,1280,320]{1,0,2:T(2,128)(2,1)}, bf16[1,1280,320]{1,0,2:T(2,128)(2,1)S(1)}) fusion(bf16[2,1280,320]{1,0,2:T(2,128)(2,1)} %all-gather.5.cloned.1.call-done), kind=kLoop, calls=%fused_computation.164 | loop fusion | bytes 3276800 | tf_op jit(solution)/shard_map/slice | solution.py:162
  68.8 34.3 %all-gather.3.cloned.1.call-done = bf16[2,320,2560]{1,2,0:T(8,128)(2,1)} async-done(((bf16[2,320,160]{1,2,0:T(8,128)(2,1)}), bf16[2,320,2560]{1,2,0:T(8,128)(2,1)}) %all-gather.3.cloned.1.call-update) | async-done | bytes 3276816 | tf_op jit(solution)/shard_map/all_gather | solution.py:156
  103.1 2.5 %fusion.1 = f32[64,2560]{1,0:T(8,128)S(1)} fusion(bf16[64,320]{1,0:T(8,128)(2,1)} %copy-done.4, bf16[2,320,2560]{1,2,0:T(8,128)(2,1)} %all-gather.3.cloned.1.call-done), kind=kOutput, calls=%fused_computation.3 | convolution fusion | flops 104857600 | bytes 2670592 | tf_op jit(solution)/shard_map/dot_general | solution.py:42
  107.0 0.7 fusion.3
  115.1 32.2 %psum.7 = f32[1,8,256]{2,0,1:T(1,128)S(1)} all-reduce(f32[1,8,256]{2,0,1:T(1,128)S(1)} %constant_dynamic-update-slice_fusion), channel_id=1, replica_groups=mesh['query'=2,'corpus'=16] {'corpus'}, use_global_device_ids=true, to_apply=%region_11.12 | all-reduce | flops 2048 | bytes 16384 | tf_op jit(solution)/shard_map/psum | solution.py:185
  147.4 6.3 %all_to_all.12 = f32[1,8,256]{2,0,1:T(1,128)S(1)} all-to-all(f32[1,8,256]{2,0,1:T(1,128)S(1)} %psum.7), channel_id=1, replica_groups=mesh['query'=2,'corpus'=16] {'query'}, dimensions={1} | all-to-all | bytes 16384 | tf_op jit(solution)/shard_map/all_to_all | solution.py:186
  153.8 0.6 fusion.11
  154.4 4.3 %all_gather.19 = bf16[2,8,256]{2,0,1:T(2,128)(2,1)S(1)} all-gather(bf16[2,4,256]{2,0,1:T(2,128)(2,1)S(1)} %fusion.11), channel_id=1, replica_groups=mesh['query'=2,'corpus'=16] {'query'}, dimensions={1}, use_global_device_ids=true | all-gather | bytes 12288 | tf_op jit(solution)/shard_map/all_gather | solution.py:190
  158.7 1.0 convolution_multiply_fusion
  (126 shorter events, 10.0 us)
Async XLA Ops:
  6.5 147.2 %copy-start = (f32[4,256,256]{2,1,0:T(8,128)S(1)}, f32[4,256,256]{2,1,0:T(8,128)}, u32[]{:S(2)}) copy-start(f32[4,256,256]{2,1,0:T(8,128)} %param.29) | copy-start | bytes 3145732
  6.5 28.4 %copy-start.12 = (bf16[2,320,20]{1,0,2:T(2,128)(2,1)S(1)}, bf16[2,320,20]{1,0,2:T(2,128)(2,1)}, u32[]{:S(2)}) copy-start(bf16[2,320,20]{1,0,2:T(2,128)(2,1)} %param.22) | copy-start | bytes 76804
  6.5 56.6 %all-gather.5.cloned.1.call-start = ((), (), s32[]{:S(2)}) async-start(), calls=%async_computation.2 | async-start | bytes 1740800 | tf_op jit(solution)/shard_map/all_gather | solution.py:157
  7.3 95.8 %all-gather.3.cloned.1.call-start = ((), (), s32[]{:S(2)}) async-start(), calls=%async_computation.1 | async-start | bytes 4177920 | tf_op jit(solution)/shard_map/all_gather | solution.py:156
  55.1 3.5 %copy-start.16 = (f32[2,320]{1,0:T(2,128)S(1)}, f32[2,320]{1,0:T(2,128)}, u32[]{:S(2)}) copy-start(f32[2,320]{1,0:T(2,128)} %param.24) | copy-start | bytes 7684
  55.1 4.1 %copy-start.17 = (f32[2,320]{1,0:T(2,128)S(1)}, f32[2,320]{1,0:T(2,128)}, u32[]{:S(2)}) copy-start(f32[2,320]{1,0:T(2,128)} %param.23) | copy-start | bytes 7684
  55.1 4.2 %copy-start.21 = (s32[1,2]{1,0:T(1,128)S(1)}, s32[1,2]{1,0:T(1,128)}, u32[]{:S(2)}) copy-start(s32[1,2]{1,0:T(1,128)} %param.18) | copy-start | bytes 28
  55.1 4.4 %copy-start.6 = (bf16[1,2,32,320]{3,2,1,0:T(8,128)(2,1)S(1)}, bf16[1,2,32,320]{3,2,1,0:T(8,128)(2,1)}, u32[]{:S(2)}) copy-start(bf16[1,2,32,320]{3,2,1,0:T(8,128)(2,1)} %param.17) | copy-start | bytes 122884
  55.1 4.4 %copy-start.11 = (bf16[1,2,32,320]{3,2,1,0:T(8,128)(2,1)S(1)}, bf16[1,2,32,320]{3,2,1,0:T(8,128)(2,1)}, u32[]{:S(2)}) copy-start(bf16[1,2,32,320]{3,2,1,0:T(8,128)(2,1)} %param.16) | copy-start | bytes 122884
  60.5 8.3 %copy-start.14 = (f32[64]{0:T(128)}, f32[64]{0:T(128)S(1)}, u32[]{:S(2)}) copy-start(f32[64]{0:T(128)S(1)} %broadcast_multiply_fusion.5) | copy-start | bytes 772
  60.7 2.4 %copy-start.18 = (f32[64]{0:T(128)}, f32[64]{0:T(128)S(1)}, u32[]{:S(2)}) copy-start(f32[64]{0:T(128)S(1)} %add_rsqrt_fusion.1) | copy-start | bytes 772
  103.1 2.9 %copy-start.10 = (bf16[2,3,320,16]{2,3,1,0:T(8,128)(2,1)S(1)}, bf16[2,3,320,16]{2,3,1,0:T(8,128)(2,1)}, u32[]{:S(2)}) copy-start(bf16[2,3,320,16]{2,3,1,0:T(8,128)(2,1)} %param.25) | copy-start | bytes 184324
  103.1 3.1 %copy-start.5 = (f32[1,2,32,320]{3,2,1,0:T(8,128)S(1)}, f32[1,2,32,320]{3,2,1,0:T(8,128)}, u32[]{:S(2)}) copy-start(f32[1,2,32,320]{3,2,1,0:T(8,128)} %get-tuple-element.14) | copy-start | bytes 245764
  103.1 3.9 %copy-start.1 = (bf16[2,320,2560]{1,2,0:T(8,128)(2,1)S(1)}, bf16[2,320,2560]{1,2,0:T(8,128)(2,1)}, u32[]{:S(2)}) copy-start(bf16[2,320,2560]{1,2,0:T(8,128)(2,1)} %all-gather.3.cloned.1.call-done) | copy-start | bytes 9830404
  105.6 1.3 copy-start.13
  106.6 1.4 copy-start.2
  107.0 1.5 copy-start.7
  109.7 0.9 copy-start.9
  109.7 1.6 copy-start.8
  110.1 2.0 %copy-start.22 = (bf16[2,2560,16]{1,2,0:T(8,128)(2,1)S(1)}, bf16[2,2560,16]{1,2,0:T(8,128)(2,1)}, u32[]{:S(2)}) copy-start(bf16[2,2560,16]{1,2,0:T(8,128)(2,1)} %param.28) | copy-start | bytes 491524
  110.3 2.2 %copy-start.15 = (f32[64]{0:T(128)S(1)}, f32[64]{0:T(128)}, u32[]{:S(2)}) copy-start(f32[64]{0:T(128)} %copy-done.14) | copy-start | bytes 772
  110.3 2.2 %copy-start.19 = (f32[64]{0:T(128)S(1)}, f32[64]{0:T(128)}, u32[]{:S(2)}) copy-start(f32[64]{0:T(128)} %copy-done.18) | copy-start | bytes 772
  112.4 46.3 %copy-start.3 = (bf16[256,2048]{1,0:T(8,128)(2,1)S(1)}, bf16[256,2048]{1,0:T(8,128)(2,1)}, u32[]{:S(2)}) copy-start(bf16[256,2048]{1,0:T(8,128)(2,1)} %param.30) | copy-start | bytes 3145732
  112.5 46.3 %copy-start.20 = (f32[256]{0:T(256)S(1)}, f32[256]{0:T(256)}, u32[]{:S(2)}) copy-start(f32[256]{0:T(256)} %param.31) | copy-start | bytes 3076
  (1 other events, 0.6 us)
Sparse Core Ops, SparseCore 0:
  9.5 43.6 all-gather.4
  55.5 47.5 all-gather.2
where the time goes:
time: 167 us
  blocking collectives  88 us (53%)
  waiting for transfers between devices  35.7 us (21%)
  between operations  13.9 us (8%)
  matrix products  13.5 us (8%)
  local copies, waits for them, and re-layouts  13.2 us (8%)
  other arithmetic  2.2 us (1%)
    all_gather x1, waiting for transfers between devices, on_device(): lax.all_gather(weight_ffin, 'corpus', axis=2, tiled=True)  34.3 us
    psum x1, blocking collectives, on_device(): totals = lax.psum(partial_grads, 'corpus')  32.2 us
    all_gather x1, blocking collectives, on_device(): lax.all_gather(weight_in, 'corpus', axis=2, tiled=True)  24.9 us
    all_gather x1, blocking collectives, on_device(): lax.all_gather(weight_out, 'corpus', axis=2, tiled=True)  20.2 us
    slice x3, local copies, waits for them, and re-layouts, fetch_forward(): return tuple((member[block] for member in gathered))  7.04 us
    all_to_all x1, blocking collectives, on_device(): lax.all_to_all(totals, 'query', split_axis=1, concat_axis=0, tiled=True)  6.35 us
    unnamed x57, local copies, waits for them, and re-layouts  4.61 us
    all_gather x1, blocking collectives, on_device(): preconditioned = lax.all_gather(owned, 'query', axis=1, tiled=True)  4.33 us
  transfers between devices with their start and end apart: 2, of which 1 were waited for; matrix products, arithmetic and copies ran while one was open for 9% of the time, Pallas kernels for 0%

commit v1 on v0

--- a/solution.py
+++ b/solution.py
@@ -183,7 +183,15 @@
             )
     partial_grads = jnp.stack(layers, axis=1)
     totals = lax.psum(partial_grads, "corpus")
-    routed = lax.all_to_all(totals, "query", split_axis=1, concat_axis=0, tiled=True)
+    routed = jnp.concatenate(
+        lax.all_to_all(
+            jnp.stack(jnp.split(totals, lax.axis_size("query"), 1), 0),
+            axis_name="query",
+            split_axis=0,
+            concat_axis=0,
+        ),
+        0,
+    )
     owned = jnp.einsum("qlk,lkj->qlj", routed, precond, precision=lax.Precision.HIGHEST).astype(
         jnp.bfloat16
     )

time: 167 us -> 167 us (level)
    unnamed x57 -> x50, local copies, waits for them, and re-layouts: 4.61 us -> 4.56 us
where the time goes in v1:
time: 167 us; the launch traced here: 166 us
  blocking collectives  88 us (53%)
  waiting for transfers between devices  35.7 us (21%)
  between operations  13.9 us (8%)
  matrix products  13.5 us (8%)
  local copies, waits for them, and re-layouts  13.2 us (8%)
  other arithmetic  2.18 us (1%)
    all_gather x1, waiting for transfers between devices, on_device(): lax.all_gather(weight_ffin, 'corpus', axis=2, tiled=True)  34.3 us
    psum x1, blocking collectives, on_device(): totals = lax.psum(partial_grads, 'corpus')  32.2 us
    all_gather x1, blocking collectives, on_device(): lax.all_gather(weight_in, 'corpus', axis=2, tiled=True)  24.9 us
    all_gather x1, blocking collectives, on_device(): lax.all_gather(weight_out, 'corpus', axis=2, tiled=True)  20.2 us
    slice x3, local copies, waits for them, and re-layouts, fetch_forward(): return tuple((member[block] for member in gathered))  7.04 us
    all_to_all x1, blocking collectives, on_device(): lax.all_to_all(jnp.stack(jnp.split(totals, lax.axis_size('query'), 1), 0)...  6.35 us
    unnamed x50, local copies, waits for them, and re-layouts  4.56 us
    all_gather x1, blocking collectives, on_device(): preconditioned = lax.all_gather(owned, 'query', axis=1, tiled=True)  4.33 us
  transfers between devices with their start and end apart: 2, of which 1 were waited for; matrix products, arithmetic and copies ran while one was open for 9% of the time, Pallas kernels for 0%

profile of v1, /device:TPU:0, one launch (start us, length us, event | category | flops | bytes accessed | tf_op | source)
XLA Modules:
  0.0 166.5 jit_solution(3436496196408009314)
XLA Ops:
  6.5 0.7 all-gather.5.cloned.1.call-update
  7.3 0.7 all-gather.3.cloned.1.call-update
  8.4 24.9 %all_gather.15 = bf16[2,320,320]{1,0,2:T(2,128)(2,1)S(1)} all-gather(bf16[2,320,20]{1,0,2:T(2,128)(2,1)} %param.19), channel_id=1, replica_groups=mesh['query'=2,'corpus'=16] {'corpus'}, dimensions={2}, use_global_device_ids=true | all-gather | bytes 435200 | tf_op jit(solution)/shard_map/all_gather | solution.py:155
  33.3 0.7 fusion.106
  34.0 0.9 copy.50
  34.9 20.2 %all_gather.18 = bf16[2,320,320]{1,0,2:T(2,128)(2,1)S(1)} all-gather(bf16[2,320,20]{1,0,2:T(2,128)(2,1)S(1)} %copy-done.12), channel_id=1, replica_groups=mesh['query'=2,'corpus'=16] {'corpus'}, dimensions={2}, use_global_device_ids=true | all-gather | bytes 435200 | tf_op jit(solution)/shard_map/all_gather | solution.py:158
  55.1 0.7 fusion.105
  55.8 0.9 copy.52
  56.7 0.9 copy.53
  57.6 0.9 copy.55
  58.6 0.6 slice_reduce_fusion.1
  59.5 0.7 fusion.103
  60.7 0.8 fusion.79
  61.7 0.6 copy-done.4
  62.3 0.8 fusion.76
  63.2 5.7 %fusion.104 = (bf16[1,1280,320]{1,0,2:T(2,128)(2,1)}, bf16[1,1280,320]{1,0,2:T(2,128)(2,1)S(1)}) fusion(bf16[2,1280,320]{1,0,2:T(2,128)(2,1)} %all-gather.5.cloned.1.call-done), kind=kLoop, calls=%fused_computation.160 | loop fusion | bytes 3276800 | tf_op jit(solution)/shard_map/slice | solution.py:162
  68.8 34.3 %all-gather.3.cloned.1.call-done = bf16[2,320,2560]{1,2,0:T(8,128)(2,1)} async-done(((bf16[2,320,160]{1,2,0:T(8,128)(2,1)}), bf16[2,320,2560]{1,2,0:T(8,128)(2,1)}) %all-gather.3.cloned.1.call-update) | async-done | bytes 3276816 | tf_op jit(solution)/shard_map/all_gather | solution.py:156
  103.1 2.5 %fusion.1 = f32[64,2560]{1,0:T(8,128)S(1)} fusion(bf16[64,320]{1,0:T(8,128)(2,1)} %copy-done.4, bf16[2,320,2560]{1,2,0:T(8,128)(2,1)} %all-gather.3.cloned.1.call-done), kind=kOutput, calls=%fused_computation.3 | convolution fusion | flops 104857600 | bytes 2670592 | tf_op jit(solution)/shard_map/dot_general | solution.py:42
  107.0 0.7 fusion.3
  115.1 32.2 %psum.7 = f32[1,8,256]{2,1,0:T(8,128)S(1)} all-reduce(f32[1,8,256]{2,1,0:T(8,128)S(1)} %stack.12), channel_id=1, replica_groups=mesh['query'=2,'corpus'=16] {'corpus'}, use_global_device_ids=true, to_apply=%region_11.12 | all-reduce | flops 2048 | bytes 16384 | tf_op jit(solution)/shard_map/psum | solution.py:185
  147.4 6.3 %all_to_all.5 = f32[2,1,4,256]{3,2,1,0:T(4,128)S(1)} all-to-all(f32[2,1,4,256]{3,2,1,0:T(4,128)S(1)} %pad_maximum_fusion.6), channel_id=1, replica_groups=mesh['query'=2,'corpus'=16] {'query'}, dimensions={0} | all-to-all | bytes 16384 | tf_op jit(solution)/shard_map/all_to_all | solution.py:187
  153.7 0.6 fusion.11
  154.3 4.3 %all_gather.19 = bf16[2,8,256]{2,0,1:T(2,128)(2,1)S(1)} all-gather(bf16[2,4,256]{2,0,1:T(2,128)(2,1)S(1)} %fusion.11), channel_id=1, replica_groups=mesh['query'=2,'corpus'=16] {'query'}, dimensions={1}, use_global_device_ids=true | all-gather | bytes 12288 | tf_op jit(solution)/shard_map/all_gather | solution.py:198
  158.7 1.0 convolution_multiply_fusion
  (119 shorter events, 10.0 us)
Async XLA Ops:
  6.5 147.2 %copy-start = (f32[4,256,256]{2,1,0:T(8,128)S(1)}, f32[4,256,256]{2,1,0:T(8,128)}, u32[]{:S(2)}) copy-start(f32[4,256,256]{2,1,0:T(8,128)} %param.29) | copy-start | bytes 3145732
  6.5 28.4 %copy-start.12 = (bf16[2,320,20]{1,0,2:T(2,128)(2,1)S(1)}, bf16[2,320,20]{1,0,2:T(2,128)(2,1)}, u32[]{:S(2)}) copy-start(bf16[2,320,20]{1,0,2:T(2,128)(2,1)} %param.22) | copy-start | bytes 76804
  6.5 56.6 %all-gather.5.cloned.1.call-start = ((), (), s32[]{:S(2)}) async-start(), calls=%async_computation.2 | async-start | bytes 1740800 | tf_op jit(solution)/shard_map/all_gather | solution.py:157
  7.3 95.8 %all-gather.3.cloned.1.call-start = ((), (), s32[]{:S(2)}) async-start(), calls=%async_computation.1 | async-start | bytes 4177920 | tf_op jit(solution)/shard_map/all_gather | solution.py:156
  55.1 3.5 %copy-start.16 = (f32[2,320]{1,0:T(2,128)S(1)}, f32[2,320]{1,0:T(2,128)}, u32[]{:S(2)}) copy-start(f32[2,320]{1,0:T(2,128)} %param.24) | copy-start | bytes 7684
  55.1 4.1 %copy-start.17 = (f32[2,320]{1,0:T(2,128)S(1)}, f32[2,320]{1,0:T(2,128)}, u32[]{:S(2)}) copy-start(f32[2,320]{1,0:T(2,128)} %param.23) | copy-start | bytes 7684
  55.1 4.2 %copy-start.21 = (s32[1,2]{1,0:T(1,128)S(1)}, s32[1,2]{1,0:T(1,128)}, u32[]{:S(2)}) copy-start(s32[1,2]{1,0:T(1,128)} %param.18) | copy-start | bytes 28
  55.1 4.4 %copy-start.6 = (bf16[1,2,32,320]{3,2,1,0:T(8,128)(2,1)S(1)}, bf16[1,2,32,320]{3,2,1,0:T(8,128)(2,1)}, u32[]{:S(2)}) copy-start(bf16[1,2,32,320]{3,2,1,0:T(8,128)(2,1)} %param.17) | copy-start | bytes 122884
  55.1 4.4 %copy-start.11 = (bf16[1,2,32,320]{3,2,1,0:T(8,128)(2,1)S(1)}, bf16[1,2,32,320]{3,2,1,0:T(8,128)(2,1)}, u32[]{:S(2)}) copy-start(bf16[1,2,32,320]{3,2,1,0:T(8,128)(2,1)} %param.16) | copy-start | bytes 122884
  60.5 8.3 %copy-start.14 = (f32[64]{0:T(128)}, f32[64]{0:T(128)S(1)}, u32[]{:S(2)}) copy-start(f32[64]{0:T(128)S(1)} %broadcast_multiply_fusion.5) | copy-start | bytes 772
  60.7 2.4 %copy-start.18 = (f32[64]{0:T(128)}, f32[64]{0:T(128)S(1)}, u32[]{:S(2)}) copy-start(f32[64]{0:T(128)S(1)} %add_rsqrt_fusion.1) | copy-start | bytes 772
  103.1 2.9 %copy-start.10 = (bf16[2,3,320,16]{2,3,1,0:T(8,128)(2,1)S(1)}, bf16[2,3,320,16]{2,3,1,0:T(8,128)(2,1)}, u32[]{:S(2)}) copy-start(bf16[2,3,320,16]{2,3,1,0:T(8,128)(2,1)} %param.25) | copy-start | bytes 184324
  103.1 3.1 %copy-start.5 = (f32[1,2,32,320]{3,2,1,0:T(8,128)S(1)}, f32[1,2,32,320]{3,2,1,0:T(8,128)}, u32[]{:S(2)}) copy-start(f32[1,2,32,320]{3,2,1,0:T(8,128)} %get-tuple-element.14) | copy-start | bytes 245764
  103.1 3.9 %copy-start.1 = (bf16[2,320,2560]{1,2,0:T(8,128)(2,1)S(1)}, bf16[2,320,2560]{1,2,0:T(8,128)(2,1)}, u32[]{:S(2)}) copy-start(bf16[2,320,2560]{1,2,0:T(8,128)(2,1)} %all-gather.3.cloned.1.call-done) | copy-start | bytes 9830404
  105.6 1.3 copy-start.13
  106.6 1.4 copy-start.2
  107.0 1.5 copy-start.7
  109.7 0.9 copy-start.9
  109.7 1.6 copy-start.8
  110.1 2.0 %copy-start.22 = (bf16[2,2560,16]{1,2,0:T(8,128)(2,1)S(1)}, bf16[2,2560,16]{1,2,0:T(8,128)(2,1)}, u32[]{:S(2)}) copy-start(bf16[2,2560,16]{1,2,0:T(8,128)(2,1)} %param.28) | copy-start | bytes 491524
  110.3 2.2 %copy-start.15 = (f32[64]{0:T(128)S(1)}, f32[64]{0:T(128)}, u32[]{:S(2)}) copy-start(f32[64]{0:T(128)} %copy-done.14) | copy-start | bytes 772
  110.3 2.2 %copy-start.19 = (f32[64]{0:T(128)S(1)}, f32[64]{0:T(128)}, u32[]{:S(2)}) copy-start(f32[64]{0:T(128)} %copy-done.18) | copy-start | bytes 772
  112.4 46.2 %copy-start.3 = (bf16[256,2048]{1,0:T(8,128)(2,1)S(1)}, bf16[256,2048]{1,0:T(8,128)(2,1)}, u32[]{:S(2)}) copy-start(bf16[256,2048]{1,0:T(8,128)(2,1)} %param.30) | copy-start | bytes 3145732
  112.5 46.2 %copy-start.20 = (f32[256]{0:T(256)S(1)}, f32[256]{0:T(256)}, u32[]{:S(2)}) copy-start(f32[256]{0:T(256)} %param.31) | copy-start | bytes 3076
  (1 other events, 0.6 us)
Sparse Core Ops, SparseCore 0:
  9.5 43.6 all-gather.4
  55.5 47.5 all-gather.2
